TPU v7x, 32 devices: a whole 2x2x4 slice. The times are simulated.
32 devices in a mesh: dp: 2 (over x), ctx: 4 (over z), tp: 4 (over y, core).
Axes of the slice: x: 2, y: 2, z: 4, core: 2. Of those that a mesh axis runs over, the one named last changes fastest.
Arguments:
- queries: bfloat16 [1024, 4096], P(('dp', 'ctx'), 'tp'), parts along dimension 0, may hold values from -25 to 25
- keys: bfloat16 [1024, 1024], P(('dp', 'ctx'), 'tp'), parts along dimension 0, may hold values from -6 to 6
- values: bfloat16 [1024, 1024], P(('dp', 'ctx'), 'tp'), parts along dimension 0, may hold values from -6 to 6
- counts: int32 [8, 4], P('dp'), parts along dimension 0, may hold values from 0 to 64, as said below
- doc_lengths: int32 [32], P('dp'), parts along dimension 0, may hold values from 1 to 256, 512 in all
Outputs:
- attended: bfloat16 [1024, 4096], P(('dp', 'ctx'), 'tp'), parts along dimension 0
There are 2 independent parts, one for each index of `dp`. A program takes and returns all parts, laid end to end along the dimension named above; each array names one. Nothing has to cross between parts.
Inputs may be any that keep to these rules, and one draw needn't show every extreme that they name: Every row and every column of counts sums to 128; no entry exceeds 64, and some entry equals 64.
All inputs are finite; a program needn't handle non-finite values.
Results may differ from a plain program's by a relative error of at most 0.006.
Values may be sent and summed in bfloat16 or wider, within the bound.
A program may use at most 64 MiB of HBM per device.

v0:
```python
import jax
import jax.numpy as jnp
from jax import lax
from jax.sharding import PartitionSpec as P

HQ = 32
KVH = 8
HD = 128


def span_pos(owner, local, half, ncx):
    return jnp.where(
        local < half, owner * half + local, (2 * ncx - 1 - owner) * half + local - half
    )


def loader_positions(counts, tok, half, ncx):
    ends = jnp.cumsum(counts, axis=1)
    starts = ends - counts
    before = jnp.cumsum(counts, axis=0) - counts
    rowids = jnp.arange(tok, dtype=jnp.int32)
    owner = jnp.sum((ends[:, None, :] <= rowids[None, :, None]).astype(jnp.int32), axis=2)
    start_sel = jnp.take_along_axis(starts, owner, axis=1)
    pre_sel = jnp.take_along_axis(before, owner, axis=1)
    return span_pos(owner, pre_sel + rowids[None, :] - start_sel, half, ncx)


def segment_of(places, doc_ends):
    return jnp.sum((doc_ends[None, :] <= places[:, None]).astype(jnp.int32), axis=1)


def make_fold(query_own, query_pos, query_seg, key_pos_all, doc_ends, kv_local, group):
    tok = query_own.shape[0]
    query_four = query_own.reshape(tok, kv_local, group, HD)
    scale = 1.0 / HD**0.5

    def attend(carry, key_rows, value_rows, key_pos):
        visible = (key_pos[None, :] <= query_pos[:, None]) & (
            segment_of(key_pos, doc_ends)[None, :] == query_seg[:, None]
        )
        count = key_rows.shape[0]
        key_three = key_rows.reshape(count, kv_local, HD)
        value_three = value_rows.reshape(count, kv_local, HD)
        top_old, total_old, accum_old = carry
        scores = (
            jnp.einsum("qcgd,kcd->cgqk", query_four, key_three, preferred_element_type=jnp.float32)
            * scale
        )
        masked = jnp.where(visible, scores, -1e30)
        top_new = jnp.maximum(top_old, jnp.max(masked, axis=-1))
        factor = jnp.exp(top_old - top_new)
        expo = jnp.where(visible, jnp.exp(masked - top_new[..., None]), 0.0)
        total_new = total_old * factor + jnp.sum(expo, axis=-1)
        weights = expo.astype(jnp.bfloat16)
        accum_new = accum_old * factor[..., None] + jnp.einsum(
            "cgqk,kcd->cgqd", weights, value_three, preferred_element_type=jnp.float32
        )
        return (top_new, total_new, accum_new)

    def fold(carry, piece, start):
        key_rows, value_rows = piece
        count = key_rows.shape[0]
        width = 512
        if width == count:
            return attend(carry, key_rows, value_rows, key_pos_all)
        blocks = count // width

        def step(state, item):
            return (attend(state, item[0], item[1], item[2]), None)

        stacked = (
            key_rows.reshape(blocks, width, key_rows.shape[1]),
            value_rows.reshape(blocks, width, value_rows.shape[1]),
            key_pos_all.reshape(blocks, width),
        )
        result, _ = lax.scan(step, carry, stacked)
        return result

    return fold


def body(queries, keys, values, counts, doc_lengths):
    ncx = lax.axis_size("ctx")
    me = lax.axis_index("ctx")
    tok = queries.shape[0]
    half = tok // 2
    slot = 2 * tok // ncx
    kv_local = keys.shape[1] // HD
    group = HQ // KVH
    ends = jnp.cumsum(counts, axis=1)
    starts = ends - counts
    column_end = jnp.cumsum(counts, axis=0)
    column_pre = column_end - counts
    my_start = jnp.take(starts, me, axis=0)
    my_count = jnp.take(counts, me, axis=0)
    offsets = jnp.arange(slot, dtype=jnp.int32)
    send_index = (my_start[:, None] + offsets[None, :]).reshape(-1)
    send_valid = (offsets[None, :] < my_count[:, None]).reshape(-1)
    send_index = jnp.clip(send_index, 0, tok - 1)
    local_ids = jnp.arange(tok, dtype=jnp.int32)
    pre_here = jnp.take(column_pre, me, axis=1)
    end_here = jnp.take(column_end, me, axis=1)
    source = jnp.sum((end_here[None, :] <= local_ids[:, None]).astype(jnp.int32), axis=1)
    recv_index = source * slot + local_ids - jnp.take(pre_here, source)
    doc_ends = jnp.cumsum(doc_lengths)
    query_pos = span_pos(me + 0 * local_ids, local_ids, half, ncx)
    query_seg = segment_of(query_pos, doc_ends)
    state = (
        jnp.full((kv_local, group, tok), -1e30, jnp.float32),
        jnp.zeros((kv_local, group, tok), jnp.float32),
        jnp.zeros((kv_local, group, tok, HD), jnp.float32),
    )
    picked = jnp.take(queries, send_index, axis=0)
    got_q = lax.all_to_all(
        jnp.where(send_valid[:, None], picked, jnp.zeros_like(picked)),
        "ctx",
        split_axis=0,
        concat_axis=0,
        tiled=True,
    )
    query_own = jnp.take(got_q, recv_index, axis=0)
    key_pos_all = loader_positions(counts, tok, half, ncx).reshape(-1)
    fold = make_fold(query_own, query_pos, query_seg, key_pos_all, doc_ends, kv_local, group)
    result = fold(
        state,
        (
            lax.all_gather(keys, "ctx", axis=0, tiled=True),
            lax.all_gather(values, "ctx", axis=0, tiled=True),
        ),
        jnp.int32(0),
    )
    top_final, total_final, accum_final = result
    mixed = accum_final / total_final[..., None]
    return (
        jnp.transpose(mixed, (2, 0, 1, 3)).reshape(tok, kv_local * group * HD).astype(jnp.bfloat16)
    )


def solution(mesh):
    placed = (
        P(("dp", "ctx"), "tp"),
        P(("dp", "ctx"), "tp"),
        P(("dp", "ctx"), "tp"),
        P("dp", None),
        P("dp"),
    )
    return jax.shard_map(
        body, mesh=mesh, in_specs=placed, out_specs=P(("dp", "ctx"), "tp"), check_vma=False
    )
```

profile of v0, /device:TPU:0, one launch (start us, length us, event | category | flops | bytes accessed | tf_op | source)
XLA Modules:
  0.0 59.8 jit_solution(13074465889589163955)
XLA Ops:
  0.0 0.0 copy-start
  0.0 0.8 %reduce_window_sum.31 = s32[4,4]{1,0:T(4,128)S(1)} reduce-window(s32[4,4]{1,0:T(4,128)} %param.14, s32[]{:T(128)} %constant.72.clone.1), window={size=4x1 pad=3_0x0_0}, to_apply=%region_0.0 | reduce-window | flops 48 | bytes 132 | tf_op jit(solution)/shard_map/jit(cumsum)/reduce_window_sum | solution.py:20
  0.8 0.9 %reduce_window_sum.32 = s32[4,4]{1,0:T(4,128)S(1)} reduce-window(s32[4,4]{1,0:T(4,128)} %param.14, s32[]{:T(128)} %constant.72.clone.1), window={size=1x4 pad=0_0x3_0}, to_apply=%region_1.2 | reduce-window | flops 48 | bytes 132 | tf_op jit(solution)/shard_map/jit(cumsum)/reduce_window_sum | solution.py:18
  1.6 0.7 %fusion.29 = (s32[4,4]{1,0:T(4,128)S(1)}, s32[4,4]{1,0:T(4,128)S(1)}) fusion(s32[4,4]{1,0:T(4,128)S(1)} %reduce_window_sum.31, s32[4,4]{1,0:T(4,128)} %param.14, s32[4,4]{1,0:T(4,128)S(1)} %reduce_window_sum.32), kind=kLoop, calls=%fused_computation.78 | loop fusion | flops 32 | bytes 320 | tf_op jit(solution)/shard_map/sub | solution.py:20
  2.3 0.7 %fusion.19 = (s32[4]{0:T(128)S(1)}, s32[4]{0:T(128)S(1)}) fusion(pred[]{:T(512)S(6)} %and.73, s32[4,4]{1,0:T(4,128)} %param.14, s32[]{:T(128)S(6)} %select_n.156, s32[4,4]{1,0:T(4,128)S(1)} %get-tuple-element.33), kind=kLoop, calls=%fused_computation.67 | loop fusion | flops 8 | bytes 69 | tf_op jit(solution)/shard_map/jit(_take)/select_n | solution.py:95
  3.0 0.1 add_clamp_fusion
  3.1 0.1 compare_and_fusion.1
  3.1 0.1 min.12
  3.2 0.1 iota_compare_fusion.1
  3.3 0.0 copy-done
  3.3 1.2 %gather_fusion = bf16[256,1024]{1,0:T(8,128)(2,1)S(1)} fusion(bf16[128,1024]{1,0:T(8,128)(2,1)S(1)} %copy-done, s32[1024]{0:T(1024)S(1)} %pad_clamp_fusion.1), kind=kCustom, calls=%fused_computation.2 | custom fusion | bytes 1049600 | tf_op jit(solution)/shard_map/jit(_take)/gather | solution.py:113
  4.5 0.9 %select_select_fusion = bf16[4,64,1024]{2,1,0:T(8,128)(2,1)} fusion(bf16[4,64,1024]{2,1,0:T(8,128)(2,1)S(1)} %bitcast.99, pred[4,64]{1,0:T(4,128)(4,1)S(1)} %compare_and_fusion.1, pred[4,64]{1,0:T(4,128)(4,1)S(1)} %iota_compare_fusion.1), kind=kLoop, calls=%fused_computation.20 | loop fusion | flops 524288 | bytes 1049088 | tf_op jit(solution)/shard_map/jit(_where)/select_n | solution.py:115
  5.4 6.3 %all-to-all-start = ((bf16[4,64,1024]{2,1,0:T(8,128)(2,1)}), bf16[4,64,1024]{2,1,0:T(8,128)(2,1)S(1)}, u32[]{:S(2)}, u32[]{:S(2)}) async-start(bf16[4,64,1024]{2,1,0:T(8,128)(2,1)} %select_select_fusion), calls=%async_computation | async-start | bytes 1048576 | tf_op jit(solution)/shard_map/all_to_all | solution.py:114
  11.7 0.2 select_reduce_fusion.1
  11.9 0.1 convert_reduce_fusion.2
  12.0 0.2 select_reduce_fusion
  12.2 0.0 copy-start.3
  12.2 0.0 copy-start.2
  12.2 0.0 copy-start.1
  12.2 4.8 %gather_fusion.2 = s32[512]{0:T(512)S(1)} fusion(s32[4,4]{1,0:T(4,128)S(1)} %get-tuple-element.32, s32[512]{0:T(512)S(1)} %fusion.18), kind=kCustom, calls=%fused_computation.clone | custom fusion | bytes 8192 | tf_op jit(solution)/shard_map/jit(take_along_axis)/gather | solution.py:24
  17.0 4.8 %gather_fusion.3 = s32[512]{0:T(512)S(1)} fusion(s32[4,4]{1,0:T(4,128)S(1)} %get-tuple-element.33, s32[512]{0:T(512)S(1)} %fusion.18), kind=kCustom, calls=%fused_computation.1.clone | custom fusion | bytes 8192 | tf_op jit(solution)/shard_map/jit(take_along_axis)/gather | solution.py:23
  21.8 0.7 %fusion.30 = (s32[1]{0:T(128)}, s32[1]{0:T(128)}, s32[1]{0:T(128)}, s32[1]{0:T(128)}) fusion(s32[4]{0:T(128)S(1)} %select_reduce_fusion), kind=kLoop, calls=%fused_computation.79 | loop fusion | bytes 32 | tf_op jit(solution)/shard_map/jit(_take)/gather | solution.py:104
  22.4 0.1 convert_reduce_fusion.3
  22.5 2.5 %fusion.23 = s32[128]{0:T(128)S(1)} fusion(s32[128]{0:T(128)S(1)} %convert_reduce_fusion.3, s32[]{:T(128)} %bitcast.12, s32[]{:T(128)} %bitcast.11, s32[]{:T(128)} %bitcast.10, s32[]{:T(128)} %bitcast.9), kind=kLoop, calls=%fused_computation.71 | loop fusion | flops 2432 | bytes 1040 | tf_op jit(solution)/shard_map/jit(_take)/jit(_where)/select_n | solution.py:121
  25.1 0.0 copy-done.3
  25.1 0.1 copy.16
  25.2 0.1 reduce
  25.3 0.0 copy-done.2
  25.4 0.1 copy.18
  25.5 13.4 %all_gather.6 = bf16[512,256]{0,1:T(8,128)(2,1)S(1)} all-gather(bf16[128,256]{0,1:T(8,128)(2,1)S(1)} %copy.18), channel_id=1, replica_groups=mesh['dp'=2,'ctx'=4,'tp'=4] {'ctx'}, dimensions={0}, use_global_device_ids=true | all-gather | bytes 327680 | tf_op jit(solution)/shard_map/all_gather | solution.py:127
  38.9 0.0 copy-done.1
  38.9 13.8 %all_gather.7 = bf16[512,256]{1,0:T(8,128)(2,1)S(1)} all-gather(bf16[128,256]{1,0:T(8,128)(2,1)S(1)} %copy-done.1), channel_id=1, replica_groups=mesh['dp'=2,'ctx'=4,'tp'=4] {'ctx'}, dimensions={0}, use_global_device_ids=true | all-gather | bytes 327680 | tf_op jit(solution)/shard_map/all_gather | solution.py:128
  52.7 0.1 copy.20
  52.9 0.1 convert_reduce_fusion.1
  53.0 0.1 convert_reduce_fusion
  53.1 2.5 %compare_and_fusion.2 = pred[128]{0:T(512)(128)(4,1)S(1)} fusion(s32[128]{0:T(128)S(1)} %convert_reduce_fusion.3, s32[]{:T(128)} %bitcast.12, s32[]{:T(128)} %bitcast.11, s32[]{:T(128)} %bitcast.10, s32[]{:T(128)} %bitcast.9), kind=kLoop, calls=%fused_computation.60 | loop fusion | flops 3200 | bytes 656 | tf_op jit(solution)/shard_map/jit(_take)/and | solution.py:121
  55.6 0.1 compare_and_fusion
  55.8 0.0 all-to-all-done
  55.8 0.9 %gather_fusion.1 = bf16[128,1024]{1,0:T(8,128)(2,1)S(1)} fusion(bf16[256,1024]{1,0:T(8,128)(2,1)S(1)} %bitcast.98, s32[1024]{0:T(1024)S(1)} %pad_clamp_fusion), kind=kCustom, calls=%fused_computation.3 | custom fusion | bytes 524800 | tf_op jit(solution)/shard_map/jit(_take)/gather | solution.py:121
  56.6 0.2 gather.32
  56.8 0.6 bitcast_reduce_fusion
  57.4 0.7 %fusion.2 = f32[2,4,128]{2,1,0:T(4,128)S(1)} fusion(f32[2,128,4,512]{3,1,2,0:T(8,128)S(1)} %get-tuple-element.39, f32[2,4,128]{2,1,0:T(4,128)S(1)} %get-tuple-element.31, pred[128,512]{1,0:T(8,128)(4,1)S(1)} %compare_and_fusion), kind=kLoop, calls=%fused_computation.9 | loop fusion | flops 2620416 | bytes 2170880 | tf_op jit(solution)/shard_map/reduce_sum | solution.py:53
  58.1 0.8 %fusion.6 = bf16[128,2,4,128]{0,3,2,1:T(8,128)(2,1)S(1)} fusion(bf16[512,2,128,1]{0,2,3,1:T(8,128)(2,1)S(1)} %bitcast.101, f32[2,128,4,512]{3,1,2,0:T(8,128)S(1)} %get-tuple-element.39, f32[2,4,128]{2,1,0:T(4,128)S(1)} %get-tuple-element.31, pred[128,512]{1,0:T(8,128)(4,1)S(1)} %compare_and_fusion, f32[128,2,4]{0,2,1:T(4,128)S(1)} %bitcast_add_fusion, ...), kind=kOutput, calls=%fused_computation.14 | convolution fusion | flops 137232384 | bytes 2699264 | tf_op jit(solution)/shard_map/cgqk,kcd->cgqd/dot_general | solution.py:55
  58.9 0.9 %copy.21 = bf16[128,1024]{1,0:T(8,128)(2,1)} copy(bf16[128,1024]{0,1:T(8,128)(2,1)S(1)} %bitcast.102) | data formatting | bytes 524288 | tf_op jit(solution)/shard_map/convert_element_type | solution.py:135
  (9 shorter events, 0.1 us)
Async XLA Ops:
  0.0 3.3 %copy-start = (bf16[128,1024]{1,0:T(8,128)(2,1)S(1)}, bf16[128,1024]{1,0:T(8,128)(2,1)}, u32[]{:S(2)}) copy-start(bf16[128,1024]{1,0:T(8,128)(2,1)} %param.11) | copy-start | bytes 786436
  5.4 50.4 %all-to-all-start = ((bf16[4,64,1024]{2,1,0:T(8,128)(2,1)}), bf16[4,64,1024]{2,1,0:T(8,128)(2,1)S(1)}, u32[]{:S(2)}, u32[]{:S(2)}) async-start(bf16[4,64,1024]{2,1,0:T(8,128)(2,1)} %select_select_fusion), calls=%async_computation | async-start | bytes 1048576 | tf_op jit(solution)/shard_map/all_to_all | solution.py:114
  12.2 12.9 %copy-start.3 = (s32[16]{0:T(128)S(1)}, s32[16]{0:T(128)}, u32[]{:S(2)}) copy-start(s32[16]{0:T(128)} %param.15) | copy-start | bytes 196
  12.2 13.1 %copy-start.2 = (bf16[128,256]{1,0:T(8,128)(2,1)S(1)}, bf16[128,256]{1,0:T(8,128)(2,1)}, u32[]{:S(2)}) copy-start(bf16[128,256]{1,0:T(8,128)(2,1)} %param.12) | copy-start | bytes 196612
  12.2 26.7 %copy-start.1 = (bf16[128,256]{1,0:T(8,128)(2,1)S(1)}, bf16[128,256]{1,0:T(8,128)(2,1)}, u32[]{:S(2)}) copy-start(bf16[128,256]{1,0:T(8,128)(2,1)} %param.13) | copy-start | bytes 196612
where the time goes:
time: 60.1 us; the launch traced here: 59.8 us
  blocking collectives  27.2 us (45%)
  local copies, waits for them, and re-layouts  13.7 us (23%)
  other arithmetic  11 us (18%)
  starting transfers between devices  6.32 us (11%)
  matrix products  1.39 us (2%)
    all_gather x1, blocking collectives, body(): lax.all_gather(values, 'ctx', axis=0, tiled=True)  13.8 us
    all_gather x1, blocking collectives, body(): lax.all_gather(keys, 'ctx', axis=0, tiled=True)  13.4 us
    all_to_all x1, starting transfers between devices, body(): lax.all_to_all(jnp.where(send_valid[:, None], picked, jnp.zeros_like(pick...  6.32 us
    gather x1, local copies, waits for them, and re-layouts, loader_positions(): pre_sel = jnp.take_along_axis(before, owner, axis=1)  4.77 us
    gather x1, local copies, waits for them, and re-layouts, loader_positions(): start_sel = jnp.take_along_axis(starts, owner, axis=1)  4.77 us
    and x1, other arithmetic, body(): query_own = jnp.take(got_q, recv_index, axis=0)  2.55 us
    select_n x1, other arithmetic, body(): query_own = jnp.take(got_q, recv_index, axis=0)  2.55 us
  transfers between devices with their start and end apart: 1, of which 0 were waited for; matrix products, arithmetic and copies ran while one was open for 28% of the time, Pallas kernels for 0%

commit v1 on v0

v1 whole, which is shorter than its diff:
```python
import functools
import math

import jax
import jax.numpy as jnp
from jax import lax
from jax.experimental import pallas as pl
from jax.experimental.pallas import tpu as pltpu
from jax.sharding import PartitionSpec as P

HQ = 32
KVH = 8
HD = 128
MESH = pl.DeviceIdType.MESH


def span_pos(owner, local, half, n):
    return jnp.where(
        local < half, owner * half + local, (2 * n - 1 - owner) * half + local - half
    )


def kernel(
    n,
    counts,
    docs,
    q_ref,
    k_ref,
    v_ref,
    out_ref,
    qsend,
    qbuf,
    kbuf,
    vbuf,
    bias,
    pick,
    qown,
    q_send_sem,
    q_recv_sem,
    kv_send_sem,
    kv_recv_sem,
):
    me = lax.axis_index("ctx")
    tok = q_ref.shape[0]
    half = tok // 2
    slot = qsend.shape[1]
    kv_local = k_ref.shape[1] // HD
    group = HQ // KVH

    barrier = pltpu.get_barrier_semaphore()
    for d in range(1, n):
        pl.semaphore_signal(
            barrier, inc=1, device_id={"ctx": lax.rem(me + d, n)}, device_id_type=MESH
        )

    row_ids = lax.broadcasted_iota(jnp.int32, (slot, tok), 1)
    row_js = lax.broadcasted_iota(jnp.int32, (slot, tok), 0)
    start = jnp.int32(0)
    for o in range(n):
        onehot = (row_ids == row_js + start).astype(jnp.bfloat16)
        qsend[o] = jnp.dot(onehot, q_ref[...], preferred_element_type=jnp.float32).astype(
            jnp.bfloat16
        )
        start = start + counts[me, o]

    pl.semaphore_wait(barrier, n - 1)

    def kv_copies(direction, d):
        sign = 1 if direction == 0 else -1
        source = me - sign * d
        target = me + sign
        result = []
        for which, (own, held) in enumerate(((k_ref, kbuf), (v_ref, vbuf))):
            result.append(
                pltpu.make_async_remote_copy(
                    src_ref=own if d == 0 else held.at[source],
                    dst_ref=held.at[source],
                    send_sem=kv_send_sem.at[which, direction, d],
                    recv_sem=kv_recv_sem.at[which, source],
                    device_id={"ctx": target},
                    device_id_type=MESH,
                )
            )
        return result

    def sends(direction, d):
        if direction == 0:
            return (me - d >= 0) & (me < n - 1)
        return (me + d < n) & (me > 0)

    def receives(direction, d):
        return (me - d >= 0) if direction == 0 else (me + d < n)

    for direction in (0, 1):

        @pl.when(sends(direction, 0))
        def _():
            for copy in kv_copies(direction, 0):
                copy.start()

    q_copies = []
    for d in range(n - 1, 0, -1):
        target = lax.rem(me + d, n)
        copy = pltpu.make_async_remote_copy(
            src_ref=qsend.at[target],
            dst_ref=qbuf.at[me],
            send_sem=q_send_sem.at[d],
            recv_sem=q_recv_sem.at[me],
            device_id={"ctx": target},
            device_id_type=MESH,
        )
        copy.start()
        q_copies.append(copy)

    qbuf[me] = qsend[me]
    kbuf[me] = k_ref[...]
    vbuf[me] = v_ref[...]

    local = lax.broadcasted_iota(jnp.int32, (tok, tok), 0)
    lane = lax.broadcasted_iota(jnp.int32, (1, tok), 1)
    query_pos = span_pos(me, local, half, n)
    doc_start = jnp.zeros((tok, tok), jnp.int32)
    end = jnp.int32(0)
    for d in range(docs.shape[0]):
        end = end + docs[d]
        doc_start = jnp.where(query_pos >= end, end, doc_start)
    before = [jnp.int32(0)] * n
    take_q = lax.broadcasted_iota(jnp.int32, (tok, slot), 0)
    take_j = lax.broadcasted_iota(jnp.int32, (tok, slot), 1)
    mine_before = jnp.int32(0)
    for l in range(n):
        start = jnp.int32(0)
        key_pos = jnp.zeros((1, tok), jnp.int32)
        for o in range(n):
            pos = span_pos(jnp.int32(o), lane + (before[o] - start), half, n)
            key_pos = jnp.where(lane >= start, pos, key_pos)
            start = start + counts[l, o]
            before[o] = before[o] + counts[l, o]
        visible = (key_pos <= query_pos) & (key_pos >= doc_start)
        bias[:, l * tok : (l + 1) * tok] = jnp.where(visible, 0.0, -1e30)
        mine = counts[l, me]
        pick[l] = ((take_q == take_j + mine_before) & (take_j < mine)).astype(jnp.bfloat16)
        mine_before = mine_before + mine

    for d in range(1, n):
        for direction in (0, 1):

            @pl.when(receives(direction, d))
            def _():
                source = me - d if direction == 0 else me + d
                for which, (own, held) in enumerate(((k_ref, kbuf), (v_ref, vbuf))):
                    pltpu.make_async_remote_copy(
                        src_ref=own,
                        dst_ref=held.at[source],
                        send_sem=kv_send_sem.at[which, direction, 0],
                        recv_sem=kv_recv_sem.at[which, source],
                        device_id={"ctx": me},
                        device_id_type=MESH,
                    ).wait_recv()

            if d < n - 1:

                @pl.when(sends(direction, d))
                def _():
                    for copy in kv_copies(direction, d):
                        copy.start()

    for d in range(1, n):
        source = lax.rem(me + d, n)
        pltpu.make_async_remote_copy(
            src_ref=qsend.at[source],
            dst_ref=qbuf.at[source],
            send_sem=q_send_sem.at[0],
            recv_sem=q_recv_sem.at[source],
            device_id={"ctx": me},
            device_id_type=MESH,
        ).wait_recv()

    own = jnp.zeros((tok, q_ref.shape[1]), jnp.float32)
    for l in range(n):
        own = own + jnp.dot(pick[l], qbuf[l], preferred_element_type=jnp.float32)
    qown[...] = own.astype(jnp.bfloat16)

    factor = math.log2(math.e) / math.sqrt(HD)
    seq = n * tok
    width = min(seq, 512)
    per = width // tok
    for c in range(kv_local):
        for g in range(group):
            h = c * group + g
            query = qown[:, h * HD : (h + 1) * HD]
            top = total = acc = None
            for b in range(seq // width):
                key = kbuf[b * per : (b + 1) * per, :, c * HD : (c + 1) * HD].reshape(width, HD)
                value = vbuf[b * per : (b + 1) * per, :, c * HD : (c + 1) * HD].reshape(width, HD)
                score = lax.dot_general(
                    query, key, (((1,), (1,)), ((), ())), preferred_element_type=jnp.float32
                )
                score = score * factor + bias[:, b * width : (b + 1) * width]
                peak = jnp.max(score, axis=1, keepdims=True)
                new = peak if b == 0 else jnp.maximum(top, peak)
                expo = jnp.exp2(score - new)
                part = jnp.sum(expo, axis=1, keepdims=True)
                mixed = jnp.dot(
                    expo.astype(jnp.bfloat16), value, preferred_element_type=jnp.float32
                )
                if b == 0:
                    total, acc = part, mixed
                else:
                    keep = jnp.exp2(top - new)
                    total = total * keep + part
                    acc = acc * keep + mixed
                top = new
            out_ref[:, h * HD : (h + 1) * HD] = (acc / total).astype(jnp.bfloat16)

    for copy in q_copies:
        copy.wait_send()
    for d in range(n - 1):
        for direction in (0, 1):

            @pl.when(sends(direction, d))
            def _():
                for copy in kv_copies(direction, d):
                    copy.wait_send()


def body(queries, keys, values, counts, doc_lengths):
    n = lax.axis_size("ctx")
    tok, wide = queries.shape
    narrow = keys.shape[1]
    slot = max(16, 2 * tok // n)
    vmem = pl.BlockSpec(memory_space=pltpu.VMEM)
    smem = pl.BlockSpec(memory_space=pltpu.SMEM)
    return pl.pallas_call(
        functools.partial(kernel, n),
        out_shape=jax.ShapeDtypeStruct((tok, wide), jnp.bfloat16),
        in_specs=[smem, smem, vmem, vmem, vmem],
        out_specs=vmem,
        scratch_shapes=[
            pltpu.VMEM((n, slot, wide), jnp.bfloat16),
            pltpu.VMEM((n, slot, wide), jnp.bfloat16),
            pltpu.VMEM((n, tok, narrow), jnp.bfloat16),
            pltpu.VMEM((n, tok, narrow), jnp.bfloat16),
            pltpu.VMEM((tok, n * tok), jnp.float32),
            pltpu.VMEM((n, tok, slot), jnp.bfloat16),
            pltpu.VMEM((tok, wide), jnp.bfloat16),
            pltpu.SemaphoreType.DMA((n,)),
            pltpu.SemaphoreType.DMA((n,)),
            pltpu.SemaphoreType.DMA((2, 2, n)),
            pltpu.SemaphoreType.DMA((2, n)),
        ],
        compiler_params=pltpu.CompilerParams(
            collective_id=0, has_side_effects=True, vmem_limit_bytes=32 * 1024 * 1024
        ),
    )(counts, doc_lengths, queries, keys, values)


def solution(mesh):
    placed = (
        P(("dp", "ctx"), "tp"),
        P(("dp", "ctx"), "tp"),
        P(("dp", "ctx"), "tp"),
        P("dp", None),
        P("dp"),
    )
    return jax.shard_map(
        body, mesh=mesh, in_specs=placed, out_specs=P(("dp", "ctx"), "tp"), check_vma=False
    )
```

time: 60.1 us -> 34.8 us (0.58)
  Pallas kernels: 0 us -> 29.9 us
  blocking collectives: 27.2 us -> 0 us
  other arithmetic: 11 us -> 0 us
  local copies, waits for them, and re-layouts: 13.7 us -> 4.67 us
  starting transfers between devices: 6.32 us -> 0 us
  matrix products: 1.39 us -> 0 us
    pallas_call x0 -> x1, Pallas kernels: none -> 29.9 us  [body(): pl.pallas_call(functools.partial(kernel, n), out_shape=jax.ShapeDtypeStru...]
    all_gather x2 -> x0, blocking collectives: 27.2 us -> none  [the longest x1 13.8 us: body(): lax.all_gather(values, 'ctx', axis=0, tiled=True)]
    gather x6 -> x0, local copies, waits for them, and re-layouts: 12.4 us -> none  [the longest x1 4.77 us: loader_positions(): pre_sel = jnp.take_along_axis(before, owner, axis=1)]
    all_to_all x1 -> x0, starting transfers between devices: 6.32 us -> none  [body(): lax.all_to_all(jnp.where(send_valid[:, None], picked, jnp.zeros_like(pick...]
    select_n x7 -> x0, other arithmetic: 4.55 us -> none  [the longest x1 2.55 us: body(): query_own = jnp.take(got_q, recv_index, axis=0)]
    unnamed x9 -> x11, local copies, waits for them, and re-layouts: 0.13 us -> 4.67 us
    and x3 -> x0, other arithmetic: 2.75 us -> none  [the longest x1 2.55 us: body(): query_own = jnp.take(got_q, recv_index, axis=0)]
    another operation x5 -> x0, other arithmetic: 1.77 us -> none  [the longest x1 0.85 us: loader_positions(): ends = jnp.cumsum(counts, axis=1)]
  transfers between devices with their start and end apart: 1 -> 0, of which waited for: 0 -> 0; matrix products, arithmetic and copies ran while one was open for 28% -> 0% of each run, Pallas kernels for 0% -> 0%
where the time goes in v1:
time: 34.8 us; the launch traced here: 34.6 us
  Pallas kernels  29.9 us (86%)
  local copies, waits for them, and re-layouts  4.67 us (13%)
    pallas_call x1, Pallas kernels, body(): pl.pallas_call(functools.partial(kernel, n), out_shape=jax.ShapeDtypeStru...  29.9 us
    unnamed x11, local copies, waits for them, and re-layouts  4.67 us

profile of v1, /device:TPU:0, one launch (start us, length us, event | category | flops | bytes accessed | tf_op | source)
XLA Modules:
  0.0 34.6 jit_solution(7067011228956879454)
XLA Ops:
  0.0 0.0 copy-start
  0.0 0.9 %copy-done = bf16[128,1024]{1,0:T(8,128)(2,1)S(1)} copy-done((bf16[128,1024]{1,0:T(8,128)(2,1)S(1)}, bf16[128,1024]{1,0:T(8,128)(2,1)}, u32[]{:S(2)}) %copy-start) | copy-done | bytes 262168
  1.0 0.0 copy-start.1
  1.0 0.8 %copy-done.1 = bf16[128,256]{1,0:T(8,128)(2,1)S(1)} copy-done((bf16[128,256]{1,0:T(8,128)(2,1)S(1)}, bf16[128,256]{1,0:T(8,128)(2,1)}, u32[]{:S(2)}) %copy-start.1) | copy-done | bytes 65560
  1.8 0.0 copy-start.2
  1.8 0.8 %copy-done.2 = bf16[128,256]{1,0:T(8,128)(2,1)S(1)} copy-done((bf16[128,256]{1,0:T(8,128)(2,1)S(1)}, bf16[128,256]{1,0:T(8,128)(2,1)}, u32[]{:S(2)}) %copy-start.2) | copy-done | bytes 65560
  2.6 0.0 copy-start.3
  2.6 0.7 %copy-done.3 = s32[4,4]{1,0:T(4,128)S(1)} copy-done((s32[4,4]{1,0:T(4,128)S(1)}, s32[4,4]{1,0:T(4,128)}, u32[]{:S(2)}) %copy-start.3) | copy-done | bytes 88
  3.3 0.0 copy-start.4
  3.3 0.7 %copy-done.4 = s32[16]{0:T(128)S(1)} copy-done((s32[16]{0:T(128)S(1)}, s32[16]{0:T(128)}, u32[]{:S(2)}) %copy-start.4) | copy-done | bytes 88
  4.0 29.9 %shard_map.55 = bf16[128,1024]{1,0:T(8,128)(2,1)S(1)} custom-call(s32[4,4]{1,0:T(4,128)S(1)} %copy-done.3, s32[16]{0:T(128)S(1)} %copy-done.4, bf16[128,1024]{1,0:T(8,128)(2,1)S(1)} %copy-done, bf16[128,256]{1,0:T(8,128)(2,1)S(1)} %copy-done.1, bf16[128,256]{1,0:T(8,128)(2,1)S(1)} %copy-done.2), custom_call_target="tpu_custom_call" | custom-call | tf_op jit(solution)/shard_map/pallas_call | solution.py:234
  33.9 0.7 %copy.7 = bf16[128,1024]{1,0:T(8,128)(2,1)} copy(bf16[128,1024]{1,0:T(8,128)(2,1)S(1)} %shard_map.55) | data formatting | bytes 524288
Async XLA Ops:
  0.0 0.9 %copy-start = (bf16[128,1024]{1,0:T(8,128)(2,1)S(1)}, bf16[128,1024]{1,0:T(8,128)(2,1)}, u32[]{:S(2)}) copy-start(bf16[128,1024]{1,0:T(8,128)(2,1)} %q_ref.1) | copy-start | bytes 786436
  1.0 0.8 %copy-start.1 = (bf16[128,256]{1,0:T(8,128)(2,1)S(1)}, bf16[128,256]{1,0:T(8,128)(2,1)}, u32[]{:S(2)}) copy-start(bf16[128,256]{1,0:T(8,128)(2,1)} %k_ref.1) | copy-start | bytes 196612
  1.8 0.8 %copy-start.2 = (bf16[128,256]{1,0:T(8,128)(2,1)S(1)}, bf16[128,256]{1,0:T(8,128)(2,1)}, u32[]{:S(2)}) copy-start(bf16[128,256]{1,0:T(8,128)(2,1)} %v_ref.1) | copy-start | bytes 196612
  2.6 0.7 %copy-start.3 = (s32[4,4]{1,0:T(4,128)S(1)}, s32[4,4]{1,0:T(4,128)}, u32[]{:S(2)}) copy-start(s32[4,4]{1,0:T(4,128)} %counts.1) | copy-start | bytes 196
  3.3 0.7 %copy-start.4 = (s32[16]{0:T(128)S(1)}, s32[16]{0:T(128)}, u32[]{:S(2)}) copy-start(s32[16]{0:T(128)} %docs.1) | copy-start | bytes 196

commit v2 on v1

--- a/solution.py
+++ b/solution.py
@@ -22,12 +22,15 @@
 
 def kernel(
     n,
+    counts_in,
+    docs_in,
+    q_in,
+    k_in,
+    v_in,
+    out_ref,
     counts,
     docs,
     q_ref,
-    k_ref,
-    v_ref,
-    out_ref,
     qsend,
     qbuf,
     kbuf,
@@ -39,12 +42,13 @@
     q_recv_sem,
     kv_send_sem,
     kv_recv_sem,
+    load_sem,
 ):
     me = lax.axis_index("ctx")
     tok = q_ref.shape[0]
     half = tok // 2
     slot = qsend.shape[1]
-    kv_local = k_ref.shape[1] // HD
+    kv_local = kbuf.shape[2] // HD
     group = HQ // KVH
 
     barrier = pltpu.get_barrier_semaphore()
@@ -52,6 +56,78 @@
         pl.semaphore_signal(
             barrier, inc=1, device_id={"ctx": lax.rem(me + d, n)}, device_id_type=MESH
         )
+
+    loads = [
+        pltpu.make_async_copy(source, target, load_sem.at[i])
+        for i, (source, target) in enumerate(
+            (
+                (k_in, kbuf.at[me]),
+                (v_in, vbuf.at[me]),
+                (counts_in, counts),
+                (docs_in, docs),
+                (q_in, q_ref),
+            )
+        )
+    ]
+    for load in loads:
+        load.start()
+
+    def kv_copies(direction, d):
+        sign = 1 if direction == 0 else -1
+        source = me - sign * d
+        target = me + sign
+        return [
+            pltpu.make_async_remote_copy(
+                src_ref=held.at[source],
+                dst_ref=held.at[source],
+                send_sem=kv_send_sem.at[which, direction, d],
+                recv_sem=kv_recv_sem.at[which, source],
+                device_id={"ctx": target},
+                device_id_type=MESH,
+            )
+            for which, held in enumerate((kbuf, vbuf))
+        ]
+
+    def sends(direction, d):
+        if direction == 0:
+            return (me - d >= 0) & (me < n - 1)
+        return (me + d < n) & (me > 0)
+
+    def receives(direction, d):
+        return (me - d >= 0) if direction == 0 else (me + d < n)
+
+    def pass_on(d):
+        for direction in (0, 1):
+
+            @pl.when(sends(direction, d))
+            def _():
+                for copy in kv_copies(direction, d):
+                    copy.start()
+
+    def q_copy(direction, d):
+        target = me + d if direction == 0 else me - d
+        return pltpu.make_async_remote_copy(
+            src_ref=qsend.at[target],
+            dst_ref=qbuf.at[me],
+            send_sem=q_send_sem.at[direction, d],
+            recv_sem=q_recv_sem.at[me],
+            device_id={"ctx": target},
+            device_id_type=MESH,
+        )
+
+    def send_q(d):
+        for direction in (0, 1):
+
+            @pl.when(receives(1 - direction, d))
+            def _():
+                q_copy(direction, d).start()
+
+    pl.semaphore_wait(barrier, n - 1)
+    loads[0].wait()
+    loads[1].wait()
+    pass_on(0)
+    for load in loads[2:]:
+        load.wait()
 
     row_ids = lax.broadcasted_iota(jnp.int32, (slot, tok), 1)
     row_js = lax.broadcasted_iota(jnp.int32, (slot, tok), 0)
@@ -63,58 +139,10 @@
         )
         start = start + counts[me, o]
 
-    pl.semaphore_wait(barrier, n - 1)
-
-    def kv_copies(direction, d):
-        sign = 1 if direction == 0 else -1
-        source = me - sign * d
-        target = me + sign
-        result = []
-        for which, (own, held) in enumerate(((k_ref, kbuf), (v_ref, vbuf))):
-            result.append(
-                pltpu.make_async_remote_copy(
-                    src_ref=own if d == 0 else held.at[source],
-                    dst_ref=held.at[source],
-                    send_sem=kv_send_sem.at[which, direction, d],
-                    recv_sem=kv_recv_sem.at[which, source],
-                    device_id={"ctx": target},
-                    device_id_type=MESH,
-                )
-            )
-        return result
-
-    def sends(direction, d):
-        if direction == 0:
-            return (me - d >= 0) & (me < n - 1)
-        return (me + d < n) & (me > 0)
-
-    def receives(direction, d):
-        return (me - d >= 0) if direction == 0 else (me + d < n)
-
-    for direction in (0, 1):
-
-        @pl.when(sends(direction, 0))
-        def _():
-            for copy in kv_copies(direction, 0):
-                copy.start()
-
-    q_copies = []
-    for d in range(n - 1, 0, -1):
-        target = lax.rem(me + d, n)
-        copy = pltpu.make_async_remote_copy(
-            src_ref=qsend.at[target],
-            dst_ref=qbuf.at[me],
-            send_sem=q_send_sem.at[d],
-            recv_sem=q_recv_sem.at[me],
-            device_id={"ctx": target},
-            device_id_type=MESH,
-        )
-        copy.start()
-        q_copies.append(copy)
+    for d in range(n - 1, 1, -1):
+        send_q(d)
 
     qbuf[me] = qsend[me]
-    kbuf[me] = k_ref[...]
-    vbuf[me] = v_ref[...]
 
     local = lax.broadcasted_iota(jnp.int32, (tok, tok), 0)
     lane = lax.broadcasted_iota(jnp.int32, (1, tok), 1)
@@ -148,9 +176,9 @@
             @pl.when(receives(direction, d))
             def _():
                 source = me - d if direction == 0 else me + d
-                for which, (own, held) in enumerate(((k_ref, kbuf), (v_ref, vbuf))):
+                for which, held in enumerate((kbuf, vbuf)):
                     pltpu.make_async_remote_copy(
-                        src_ref=own,
+                        src_ref=held.at[source],
                         dst_ref=held.at[source],
                         send_sem=kv_send_sem.at[which, direction, 0],
                         recv_sem=kv_recv_sem.at[which, source],
@@ -158,19 +186,17 @@
                         device_id_type=MESH,
                     ).wait_recv()
 
-            if d < n - 1:
-
-                @pl.when(sends(direction, d))
-                def _():
-                    for copy in kv_copies(direction, d):
-                        copy.start()
+        if d < n - 1:
+            pass_on(d)
+        if d == 1:
+            send_q(1)
 
     for d in range(1, n):
         source = lax.rem(me + d, n)
         pltpu.make_async_remote_copy(
             src_ref=qsend.at[source],
             dst_ref=qbuf.at[source],
-            send_sem=q_send_sem.at[0],
+            send_sem=q_send_sem.at[0, 0],
             recv_sem=q_recv_sem.at[source],
             device_id={"ctx": me},
             device_id_type=MESH,
@@ -213,8 +239,13 @@
                 top = new
             out_ref[:, h * HD : (h + 1) * HD] = (acc / total).astype(jnp.bfloat16)
 
-    for copy in q_copies:
-        copy.wait_send()
+    for d in range(1, n):
+        for direction in (0, 1):
+
+            @pl.when(receives(1 - direction, d))
+            def _():
+                q_copy(direction, d).wait_send()
+
     for d in range(n - 1):
         for direction in (0, 1):
 
@@ -230,13 +261,16 @@
     narrow = keys.shape[1]
     slot = max(16, 2 * tok // n)
     vmem = pl.BlockSpec(memory_space=pltpu.VMEM)
-    smem = pl.BlockSpec(memory_space=pltpu.SMEM)
+    anywhere = pl.BlockSpec(memory_space=pl.ANY)
     return pl.pallas_call(
         functools.partial(kernel, n),
         out_shape=jax.ShapeDtypeStruct((tok, wide), jnp.bfloat16),
-        in_specs=[smem, smem, vmem, vmem, vmem],
+        in_specs=[anywhere] * 5,
         out_specs=vmem,
         scratch_shapes=[
+            pltpu.SMEM(counts.shape, jnp.int32),
+            pltpu.SMEM(doc_lengths.shape, jnp.int32),
+            pltpu.VMEM((tok, wide), jnp.bfloat16),
             pltpu.VMEM((n, slot, wide), jnp.bfloat16),
             pltpu.VMEM((n, slot, wide), jnp.bfloat16),
             pltpu.VMEM((n, tok, narrow), jnp.bfloat16),
@@ -244,13 +278,14 @@
             pltpu.VMEM((tok, n * tok), jnp.float32),
             pltpu.VMEM((n, tok, slot), jnp.bfloat16),
             pltpu.VMEM((tok, wide), jnp.bfloat16),
-            pltpu.SemaphoreType.DMA((n,)),
+            pltpu.SemaphoreType.DMA((2, n)),
             pltpu.SemaphoreType.DMA((n,)),
             pltpu.SemaphoreType.DMA((2, 2, n)),
             pltpu.SemaphoreType.DMA((2, n)),
+            pltpu.SemaphoreType.DMA((5,)),
         ],
         compiler_params=pltpu.CompilerParams(
-            collective_id=0, has_side_effects=True, vmem_limit_bytes=32 * 1024 * 1024
+            collective_id=0, has_side_effects=True, vmem_limit_bytes=56 * 1024 * 1024
         ),
     )(counts, doc_lengths, queries, keys, values)
 

time: 34.8 us -> 30.2 us (0.87)
  local copies, waits for them, and re-layouts: 4.67 us -> 1.67 us
  Pallas kernels: 29.9 us -> 28.3 us
    unnamed x11 -> x1, local copies, waits for them, and re-layouts: 4.67 us -> 1.67 us
    pallas_call x1, Pallas kernels: 29.9 us -> 28.3 us  [body(): pl.pallas_call(functools.partial(kernel, n), out_shape=jax.ShapeDtypeStru...]
where the time goes in v2:
time: 30.2 us; the launch traced here: 30 us
  Pallas kernels  28.3 us (94%)
  local copies, waits for them, and re-layouts  1.67 us (6%)
    pallas_call x1, Pallas kernels, body(): pl.pallas_call(functools.partial(kernel, n), out_shape=jax.ShapeDtypeStru...  28.3 us
    unnamed x1, local copies, waits for them, and re-layouts  1.67 us

profile of v2, /device:TPU:0, one launch (start us, length us, event | category | flops | bytes accessed | tf_op | source)
XLA Modules:
  0.0 30.0 jit_solution(3943427278505552261)
XLA Ops:
  0.0 28.3 %shard_map.55 = bf16[128,1024]{1,0:T(8,128)(2,1)} custom-call(s32[4,4]{1,0:T(4,128)} %counts_in.1, s32[16]{0:T(128)} %docs_in.1, bf16[128,1024]{1,0:T(8,128)(2,1)} %q_in.1, bf16[128,256]{1,0:T(8,128)(2,1)} %k_in.1, bf16[128,256]{1,0:T(8,128)(2,1)} %v_in.1), custom_call_target="tpu_custom_call" | custom-call | tf_op jit(solution)/shard_map/pallas_call | solution.py:265
  28.4 1.7 %copy.7 = bf16[128,1024]{1,0:T(8,128)(2,1)} copy(bf16[128,1024]{1,0:T(8,128)(2,1)} %shard_map.55) | data formatting | bytes 524288

commit v3 on v2

--- a/solution.py
+++ b/solution.py
@@ -11,6 +11,7 @@
 HQ = 32
 KVH = 8
 HD = 128
+PART = 2 * HD
 MESH = pl.DeviceIdType.MESH
 
 
@@ -37,7 +38,6 @@
     vbuf,
     bias,
     pick,
-    qown,
     q_send_sem,
     q_recv_sem,
     kv_send_sem,
@@ -47,8 +47,8 @@
     me = lax.axis_index("ctx")
     tok = q_ref.shape[0]
     half = tok // 2
-    slot = qsend.shape[1]
-    kv_local = kbuf.shape[2] // HD
+    slot = qsend.shape[2]
+    parts = q_ref.shape[1] // PART
     group = HQ // KVH
 
     barrier = pltpu.get_barrier_semaphore()
@@ -96,31 +96,46 @@
     def receives(direction, d):
         return (me - d >= 0) if direction == 0 else (me + d < n)
 
+    def wait_kv(direction, d):
+        source = me - d if direction == 0 else me + d
+        for which, held in enumerate((kbuf, vbuf)):
+            pltpu.make_async_remote_copy(
+                src_ref=held.at[source],
+                dst_ref=held.at[source],
+                send_sem=kv_send_sem.at[which, direction, 0],
+                recv_sem=kv_recv_sem.at[which, source],
+                device_id={"ctx": me},
+                device_id_type=MESH,
+            ).wait_recv()
+
     def pass_on(d):
         for direction in (0, 1):
 
             @pl.when(sends(direction, d))
             def _():
+                if d > 0:
+                    wait_kv(direction, d)
                 for copy in kv_copies(direction, d):
                     copy.start()
 
-    def q_copy(direction, d):
+    def q_copy(direction, d, p):
         target = me + d if direction == 0 else me - d
         return pltpu.make_async_remote_copy(
-            src_ref=qsend.at[target],
-            dst_ref=qbuf.at[me],
-            send_sem=q_send_sem.at[direction, d],
-            recv_sem=q_recv_sem.at[me],
+            src_ref=qsend.at[p, target],
+            dst_ref=qbuf.at[p, me],
+            send_sem=q_send_sem.at[p, direction, d],
+            recv_sem=q_recv_sem.at[p, me],
             device_id={"ctx": target},
             device_id_type=MESH,
         )
 
-    def send_q(d):
-        for direction in (0, 1):
-
-            @pl.when(receives(1 - direction, d))
-            def _():
-                q_copy(direction, d).start()
+    def send_q(p):
+        for d in range(n - 1, 0, -1):
+            for direction in (0, 1):
+
+                @pl.when(receives(1 - direction, d))
+                def _():
+                    q_copy(direction, d, p).start()
 
     pl.semaphore_wait(barrier, n - 1)
     loads[0].wait()
@@ -132,17 +147,31 @@
     row_ids = lax.broadcasted_iota(jnp.int32, (slot, tok), 1)
     row_js = lax.broadcasted_iota(jnp.int32, (slot, tok), 0)
     start = jnp.int32(0)
+    onehots = []
     for o in range(n):
-        onehot = (row_ids == row_js + start).astype(jnp.bfloat16)
-        qsend[o] = jnp.dot(onehot, q_ref[...], preferred_element_type=jnp.float32).astype(
-            jnp.bfloat16
+        onehots.append((row_ids == row_js + start).astype(jnp.bfloat16))
+        start = start + counts[me, o]
+    onehot = jnp.concatenate(onehots, axis=0)
+
+    def pack_q(p):
+        packed = jnp.dot(
+            onehot, q_ref[:, p * PART : (p + 1) * PART], preferred_element_type=jnp.float32
         )
-        start = start + counts[me, o]
-
-    for d in range(n - 1, 1, -1):
-        send_q(d)
-
-    qbuf[me] = qsend[me]
+        qsend[p] = packed.astype(jnp.bfloat16).reshape(n, slot, PART)
+        qbuf[p, me] = qsend[p, me]
+
+    for p in range(parts):
+        pack_q(p)
+        if p == 0:
+            send_q(0)
+    sent = 1
+    for d in range(1, n - 1):
+        pass_on(d)
+        if sent < parts:
+            send_q(sent)
+            sent += 1
+    for p in range(sent, parts):
+        send_q(p)
 
     local = lax.broadcasted_iota(jnp.int32, (tok, tok), 0)
     lane = lax.broadcasted_iota(jnp.int32, (1, tok), 1)
@@ -153,8 +182,9 @@
         end = end + docs[d]
         doc_start = jnp.where(query_pos >= end, end, doc_start)
     before = [jnp.int32(0)] * n
-    take_q = lax.broadcasted_iota(jnp.int32, (tok, slot), 0)
-    take_j = lax.broadcasted_iota(jnp.int32, (tok, slot), 1)
+    take_q = lax.broadcasted_iota(jnp.int32, (tok, n * slot), 0)
+    take_row = lax.broadcasted_iota(jnp.int32, (1, n * slot), 1)
+    take = jnp.full((1, n * slot), -1, jnp.int32)
     mine_before = jnp.int32(0)
     for l in range(n):
         start = jnp.int32(0)
@@ -167,54 +197,39 @@
         visible = (key_pos <= query_pos) & (key_pos >= doc_start)
         bias[:, l * tok : (l + 1) * tok] = jnp.where(visible, 0.0, -1e30)
         mine = counts[l, me]
-        pick[l] = ((take_q == take_j + mine_before) & (take_j < mine)).astype(jnp.bfloat16)
+        j = take_row - l * slot
+        take = jnp.where((j >= 0) & (j < mine), j + mine_before, take)
         mine_before = mine_before + mine
+    pick[...] = (take_q == take).astype(jnp.bfloat16)
 
     for d in range(1, n):
         for direction in (0, 1):
 
-            @pl.when(receives(direction, d))
+            @pl.when(receives(direction, d) & jnp.logical_not(sends(direction, d)))
             def _():
-                source = me - d if direction == 0 else me + d
-                for which, held in enumerate((kbuf, vbuf)):
-                    pltpu.make_async_remote_copy(
-                        src_ref=held.at[source],
-                        dst_ref=held.at[source],
-                        send_sem=kv_send_sem.at[which, direction, 0],
-                        recv_sem=kv_recv_sem.at[which, source],
-                        device_id={"ctx": me},
-                        device_id_type=MESH,
-                    ).wait_recv()
-
-        if d < n - 1:
-            pass_on(d)
-        if d == 1:
-            send_q(1)
-
-    for d in range(1, n):
-        source = lax.rem(me + d, n)
-        pltpu.make_async_remote_copy(
-            src_ref=qsend.at[source],
-            dst_ref=qbuf.at[source],
-            send_sem=q_send_sem.at[0, 0],
-            recv_sem=q_recv_sem.at[source],
-            device_id={"ctx": me},
-            device_id_type=MESH,
-        ).wait_recv()
-
-    own = jnp.zeros((tok, q_ref.shape[1]), jnp.float32)
-    for l in range(n):
-        own = own + jnp.dot(pick[l], qbuf[l], preferred_element_type=jnp.float32)
-    qown[...] = own.astype(jnp.bfloat16)
+                wait_kv(direction, d)
 
     factor = math.log2(math.e) / math.sqrt(HD)
     seq = n * tok
     width = min(seq, 512)
     per = width // tok
-    for c in range(kv_local):
-        for g in range(group):
-            h = c * group + g
-            query = qown[:, h * HD : (h + 1) * HD]
+    for p in range(parts):
+        for d in range(1, n):
+            source = lax.rem(me + d, n)
+            pltpu.make_async_remote_copy(
+                src_ref=qsend.at[p, source],
+                dst_ref=qbuf.at[p, source],
+                send_sem=q_send_sem.at[0, 0, 0],
+                recv_sem=q_recv_sem.at[p, source],
+                device_id={"ctx": me},
+                device_id_type=MESH,
+            ).wait_recv()
+        own = jnp.dot(
+            pick[...], qbuf[p].reshape(n * slot, PART), preferred_element_type=jnp.float32
+        ).astype(jnp.bfloat16)
+        for h in range(p * PART // HD, (p + 1) * PART // HD):
+            c = h // group
+            query = own[:, h * HD - p * PART : (h + 1) * HD - p * PART]
             top = total = acc = None
             for b in range(seq // width):
                 key = kbuf[b * per : (b + 1) * per, :, c * HD : (c + 1) * HD].reshape(width, HD)
@@ -244,7 +259,8 @@
 
             @pl.when(receives(1 - direction, d))
             def _():
-                q_copy(direction, d).wait_send()
+                for p in range(parts):
+                    q_copy(direction, d, p).wait_send()
 
     for d in range(n - 1):
         for direction in (0, 1):
@@ -260,26 +276,26 @@
     tok, wide = queries.shape
     narrow = keys.shape[1]
     slot = max(16, 2 * tok // n)
+    parts = wide // PART
     vmem = pl.BlockSpec(memory_space=pltpu.VMEM)
     anywhere = pl.BlockSpec(memory_space=pl.ANY)
     return pl.pallas_call(
         functools.partial(kernel, n),
-        out_shape=jax.ShapeDtypeStruct((tok, wide), jnp.bfloat16),
+        out_shape=pltpu.VMEM((tok, wide), jnp.bfloat16),
         in_specs=[anywhere] * 5,
         out_specs=vmem,
         scratch_shapes=[
             pltpu.SMEM(counts.shape, jnp.int32),
             pltpu.SMEM(doc_lengths.shape, jnp.int32),
             pltpu.VMEM((tok, wide), jnp.bfloat16),
-            pltpu.VMEM((n, slot, wide), jnp.bfloat16),
-            pltpu.VMEM((n, slot, wide), jnp.bfloat16),
+            pltpu.VMEM((parts, n, slot, PART), jnp.bfloat16),
+            pltpu.VMEM((parts, n, slot, PART), jnp.bfloat16),
             pltpu.VMEM((n, tok, narrow), jnp.bfloat16),
             pltpu.VMEM((n, tok, narrow), jnp.bfloat16),
             pltpu.VMEM((tok, n * tok), jnp.float32),
-            pltpu.VMEM((n, tok, slot), jnp.bfloat16),
-            pltpu.VMEM((tok, wide), jnp.bfloat16),
-            pltpu.SemaphoreType.DMA((2, n)),
-            pltpu.SemaphoreType.DMA((n,)),
+            pltpu.VMEM((tok, n * slot), jnp.bfloat16),
+            pltpu.SemaphoreType.DMA((parts, 2, n)),
+            pltpu.SemaphoreType.DMA((parts, n)),
             pltpu.SemaphoreType.DMA((2, 2, n)),
             pltpu.SemaphoreType.DMA((2, n)),
             pltpu.SemaphoreType.DMA((5,)),

time: 30.2 us -> 29.4 us (0.974)
  local copies, waits for them, and re-layouts: 1.67 us -> 0.71 us
    unnamed x1, local copies, waits for them, and re-layouts: 1.67 us -> 0.71 us
where the time goes in v3:
time: 29.4 us; the launch traced here: 29.2 us
  Pallas kernels  28.5 us (97%)
  local copies, waits for them, and re-layouts  0.71 us (2%)
    pallas_call x1, Pallas kernels, body(): pl.pallas_call(functools.partial(kernel, n), out_shape=pltpu.VMEM((tok, w...  28.5 us
    unnamed x1, local copies, waits for them, and re-layouts  0.71 us

profile of v3, /device:TPU:0, one launch (start us, length us, event | category | flops | bytes accessed | tf_op | source)
XLA Modules:
  0.0 29.2 jit_solution(12359105489541422349)
XLA Ops:
  0.0 28.5 %shard_map.55 = bf16[128,1024]{1,0:T(8,128)(2,1)S(1)} custom-call(s32[4,4]{1,0:T(4,128)} %counts_in.1, s32[16]{0:T(128)} %docs_in.1, bf16[128,1024]{1,0:T(8,128)(2,1)} %q_in.1, bf16[128,256]{1,0:T(8,128)(2,1)} %k_in.1, bf16[128,256]{1,0:T(8,128)(2,1)} %v_in.1), custom_call_target="tpu_custom_call" | custom-call | tf_op jit(solution)/shard_map/pallas_call | solution.py:282
  28.5 0.7 %copy.7 = bf16[128,1024]{1,0:T(8,128)(2,1)} copy(bf16[128,1024]{1,0:T(8,128)(2,1)S(1)} %shard_map.55) | data formatting | bytes 524288

commit v4 on v3

--- a/solution.py
+++ b/solution.py
@@ -129,13 +129,26 @@
             device_id_type=MESH,
         )
 
-    def send_q(p):
-        for d in range(n - 1, 0, -1):
+    def at_end(direction, d):
+        return (me + d == n - 1) if direction == 0 else (me - d == 0)
+
+    def send_q_ends():
+        for p in range(parts):
+            for d in range(n - 1, 0, -1):
+                for direction in (0, 1):
+
+                    @pl.when(at_end(direction, d))
+                    def _():
+                        q_copy(direction, d, p).start()
+
+    def send_q_rest():
+        for d in range(1, n):
             for direction in (0, 1):
 
-                @pl.when(receives(1 - direction, d))
+                @pl.when(receives(1 - direction, d) & jnp.logical_not(at_end(direction, d)))
                 def _():
-                    q_copy(direction, d, p).start()
+                    for p in range(parts):
+                        q_copy(direction, d, p).start()
 
     pl.semaphore_wait(barrier, n - 1)
     loads[0].wait()
@@ -162,16 +175,7 @@
 
     for p in range(parts):
         pack_q(p)
-        if p == 0:
-            send_q(0)
-    sent = 1
-    for d in range(1, n - 1):
-        pass_on(d)
-        if sent < parts:
-            send_q(sent)
-            sent += 1
-    for p in range(sent, parts):
-        send_q(p)
+    send_q_ends()
 
     local = lax.broadcasted_iota(jnp.int32, (tok, tok), 0)
     lane = lax.broadcasted_iota(jnp.int32, (1, tok), 1)
@@ -201,6 +205,13 @@
         take = jnp.where((j >= 0) & (j < mine), j + mine_before, take)
         mine_before = mine_before + mine
     pick[...] = (take_q == take).astype(jnp.bfloat16)
+
+    for d in range(1, n - 1):
+        pass_on(d)
+        if d == 1:
+            send_q_rest()
+    if n < 3:
+        send_q_rest()
 
     for d in range(1, n):
         for direction in (0, 1):

time: 29.4 us -> 29.5 us (level)
  no operation moved by 1% of the time
where the time goes in v4:
time: 29.5 us; the launch traced here: 29.3 us
  Pallas kernels  28.6 us (97%)
  local copies, waits for them, and re-layouts  0.71 us (2%)
    pallas_call x1, Pallas kernels, body(): pl.pallas_call(functools.partial(kernel, n), out_shape=pltpu.VMEM((tok, w...  28.6 us
    unnamed x1, local copies, waits for them, and re-layouts  0.71 us

profile of v4, /device:TPU:0, one launch (start us, length us, event | category | flops | bytes accessed | tf_op | source)
XLA Modules:
  0.0 29.3 jit_solution(5943633990019414407)
XLA Ops:
  0.0 28.6 %shard_map.55 = bf16[128,1024]{1,0:T(8,128)(2,1)S(1)} custom-call(s32[4,4]{1,0:T(4,128)} %counts_in.1, s32[16]{0:T(128)} %docs_in.1, bf16[128,1024]{1,0:T(8,128)(2,1)} %q_in.1, bf16[128,256]{1,0:T(8,128)(2,1)} %k_in.1, bf16[128,256]{1,0:T(8,128)(2,1)} %v_in.1), custom_call_target="tpu_custom_call" | custom-call | tf_op jit(solution)/shard_map/pallas_call | solution.py:293
  28.6 0.7 %copy.7 = bf16[128,1024]{1,0:T(8,128)(2,1)} copy(bf16[128,1024]{1,0:T(8,128)(2,1)S(1)} %shard_map.55) | data formatting | bytes 524288

commit v5 on v4

--- a/solution.py
+++ b/solution.py
@@ -38,11 +38,19 @@
     vbuf,
     bias,
     pick,
+    rbuf,
+    rpick,
+    merged,
+    obuf,
+    own,
     q_send_sem,
     q_recv_sem,
     kv_send_sem,
     kv_recv_sem,
     load_sem,
+    r_recv_sem,
+    o_send_sem,
+    o_recv_sem,
 ):
     me = lax.axis_index("ctx")
     tok = q_ref.shape[0]
@@ -50,6 +58,9 @@
     slot = qsend.shape[2]
     parts = q_ref.shape[1] // PART
     group = HQ // KVH
+    is_end = (me == 0) | (me == n - 1)
+    is_relay = (me == 1) | (me == n - 2)
+    end_id = jnp.where(me == 1, 0, n - 1)
 
     barrier = pltpu.get_barrier_semaphore()
     for d in range(1, n):
@@ -132,14 +143,54 @@
     def at_end(direction, d):
         return (me + d == n - 1) if direction == 0 else (me - d == 0)
 
+    def end_copy(direction, d, p):
+        return pltpu.make_async_remote_copy(
+            src_ref=qsend.at[p, n - 1 if direction == 0 else 0],
+            dst_ref=rbuf.at[p, me],
+            send_sem=q_send_sem.at[p, direction, d],
+            recv_sem=r_recv_sem.at[p, me],
+            device_id={"ctx": n - 2 if direction == 0 else 1},
+            device_id_type=MESH,
+        )
+
+    def merged_copy(p):
+        return pltpu.make_async_remote_copy(
+            src_ref=merged.at[p],
+            dst_ref=obuf.at[p],
+            send_sem=o_send_sem.at[p],
+            recv_sem=o_recv_sem.at[p],
+            device_id={"ctx": end_id},
+            device_id_type=MESH,
+        )
+
+    def merge(p):
+        for d in range(1, n):
+            source = lax.rem(me + d, n)
+
+            @pl.when(source != end_id)
+            def _():
+                pltpu.make_async_remote_copy(
+                    src_ref=rbuf.at[p, source],
+                    dst_ref=rbuf.at[p, source],
+                    send_sem=q_send_sem.at[0, 0, 0],
+                    recv_sem=r_recv_sem.at[p, source],
+                    device_id={"ctx": me},
+                    device_id_type=MESH,
+                ).wait_recv()
+
+        merged[p] = jnp.dot(
+            rpick[...], rbuf[p].reshape(n * slot, PART), preferred_element_type=jnp.float32
+        ).astype(jnp.bfloat16)
+        merged_copy(p).start()
+
     def send_q_ends():
         for p in range(parts):
-            for d in range(n - 1, 0, -1):
+            for d in range(n - 1, 1, -1):
                 for direction in (0, 1):
 
                     @pl.when(at_end(direction, d))
                     def _():
-                        q_copy(direction, d, p).start()
+                        end_copy(direction, d, p).start()
 
     def send_q_rest():
         for d in range(1, n):
@@ -171,11 +222,23 @@
             onehot, q_ref[:, p * PART : (p + 1) * PART], preferred_element_type=jnp.float32
         )
         qsend[p] = packed.astype(jnp.bfloat16).reshape(n, slot, PART)
-        qbuf[p, me] = qsend[p, me]
 
     for p in range(parts):
         pack_q(p)
     send_q_ends()
+
+    @pl.when(is_end)
+    def _():
+        qbuf[...] = jnp.zeros_like(qbuf)
+
+    @pl.when(is_relay)
+    def _():
+        for p in range(parts):
+            rbuf[p, me] = qsend[p, end_id]
+            rbuf[p, end_id] = jnp.zeros((slot, PART), jnp.bfloat16)
+
+    for p in range(parts):
+        qbuf[p, me] = qsend[p, me]
 
     local = lax.broadcasted_iota(jnp.int32, (tok, tok), 0)
     lane = lax.broadcasted_iota(jnp.int32, (1, tok), 1)
@@ -190,6 +253,8 @@
     take_row = lax.broadcasted_iota(jnp.int32, (1, n * slot), 1)
     take = jnp.full((1, n * slot), -1, jnp.int32)
     mine_before = jnp.int32(0)
+    end_take = take
+    end_before = jnp.int32(0)
     for l in range(n):
         start = jnp.int32(0)
         key_pos = jnp.zeros((1, tok), jnp.int32)
@@ -204,14 +269,21 @@
         j = take_row - l * slot
         take = jnp.where((j >= 0) & (j < mine), j + mine_before, take)
         mine_before = mine_before + mine
+        theirs = counts[l, end_id]
+        end_take = jnp.where((j >= 0) & (j < theirs), j + end_before, end_take)
+        end_before = end_before + theirs
     pick[...] = (take_q == take).astype(jnp.bfloat16)
+    rpick[...] = (take_q == end_take).astype(jnp.bfloat16)
 
     for d in range(1, n - 1):
         pass_on(d)
         if d == 1:
             send_q_rest()
-    if n < 3:
-        send_q_rest()
+
+    @pl.when(is_relay)
+    def _():
+        for p in range(parts):
+            merge(p)
 
     for d in range(1, n):
         for direction in (0, 1):
@@ -225,19 +297,28 @@
     width = min(seq, 512)
     per = width // tok
     for p in range(parts):
-        for d in range(1, n):
-            source = lax.rem(me + d, n)
-            pltpu.make_async_remote_copy(
-                src_ref=qsend.at[p, source],
-                dst_ref=qbuf.at[p, source],
-                send_sem=q_send_sem.at[0, 0, 0],
-                recv_sem=q_recv_sem.at[p, source],
-                device_id={"ctx": me},
-                device_id_type=MESH,
-            ).wait_recv()
-        own = jnp.dot(
+        @pl.when(jnp.logical_not(is_end))
+        def _():
+            for d in range(1, n):
+                source = lax.rem(me + d, n)
+                pltpu.make_async_remote_copy(
+                    src_ref=qsend.at[p, source],
+                    dst_ref=qbuf.at[p, source],
+                    send_sem=q_send_sem.at[0, 0, 0],
+                    recv_sem=q_recv_sem.at[p, source],
+                    device_id={"ctx": me},
+                    device_id_type=MESH,
+                ).wait_recv()
+
+        own[...] = jnp.dot(
             pick[...], qbuf[p].reshape(n * slot, PART), preferred_element_type=jnp.float32
         ).astype(jnp.bfloat16)
+
+        @pl.when(is_end)
+        def _():
+            merged_copy(p).wait_recv()
+            own[...] = own[...] + obuf[p]
+
         for h in range(p * PART // HD, (p + 1) * PART // HD):
             c = h // group
             query = own[:, h * HD - p * PART : (h + 1) * HD - p * PART]
@@ -268,10 +349,22 @@
     for d in range(1, n):
         for direction in (0, 1):
 
-            @pl.when(receives(1 - direction, d))
+            @pl.when(receives(1 - direction, d) & jnp.logical_not(at_end(direction, d)))
             def _():
                 for p in range(parts):
                     q_copy(direction, d, p).wait_send()
+
+            if d > 1:
+
+                @pl.when(at_end(direction, d))
+                def _():
+                    for p in range(parts):
+                        end_copy(direction, d, p).wait_send()
+
+    @pl.when(is_relay)
+    def _():
+        for p in range(parts):
+            merged_copy(p).wait_send()
 
     for d in range(n - 1):
         for direction in (0, 1):
@@ -305,11 +398,19 @@
             pltpu.VMEM((n, tok, narrow), jnp.bfloat16),
             pltpu.VMEM((tok, n * tok), jnp.float32),
             pltpu.VMEM((tok, n * slot), jnp.bfloat16),
+            pltpu.VMEM((parts, n, slot, PART), jnp.bfloat16),
+            pltpu.VMEM((tok, n * slot), jnp.bfloat16),
+            pltpu.VMEM((parts, tok, PART), jnp.bfloat16),
+            pltpu.VMEM((parts, tok, PART), jnp.bfloat16),
+            pltpu.VMEM((tok, PART), jnp.bfloat16),
             pltpu.SemaphoreType.DMA((parts, 2, n)),
             pltpu.SemaphoreType.DMA((parts, n)),
             pltpu.SemaphoreType.DMA((2, 2, n)),
             pltpu.SemaphoreType.DMA((2, n)),
             pltpu.SemaphoreType.DMA((5,)),
+            pltpu.SemaphoreType.DMA((parts, n)),
+            pltpu.SemaphoreType.DMA((parts,)),
+            pltpu.SemaphoreType.DMA((parts,)),
         ],
         compiler_params=pltpu.CompilerParams(
             collective_id=0, has_side_effects=True, vmem_limit_bytes=56 * 1024 * 1024

time: 29.5 us -> 31.9 us (1.081)
  Pallas kernels: 28.6 us -> 31 us
    pallas_call x1, Pallas kernels: 28.6 us -> 31 us  [body(): pl.pallas_call(functools.partial(kernel, n), out_shape=pltpu.VMEM((tok, w...]
where the time goes in v5:
time: 31.9 us; the launch traced here: 31.7 us
  Pallas kernels  31 us (97%)
  local copies, waits for them, and re-layouts  0.71 us (2%)
    pallas_call x1, Pallas kernels, body(): pl.pallas_call(functools.partial(kernel, n), out_shape=pltpu.VMEM((tok, w...  31 us
    unnamed x1, local copies, waits for them, and re-layouts  0.71 us

profile of v5, /device:TPU:0, one launch (start us, length us, event | category | flops | bytes accessed | tf_op | source)
XLA Modules:
  0.0 31.7 jit_solution(2845588594772542967)
XLA Ops:
  0.0 31.0 %shard_map.55 = bf16[128,1024]{1,0:T(8,128)(2,1)S(1)} custom-call(s32[4,4]{1,0:T(4,128)} %counts_in.1, s32[16]{0:T(128)} %docs_in.1, bf16[128,1024]{1,0:T(8,128)(2,1)} %q_in.1, bf16[128,256]{1,0:T(8,128)(2,1)} %k_in.1, bf16[128,256]{1,0:T(8,128)(2,1)} %v_in.1), custom_call_target="tpu_custom_call" | custom-call | tf_op jit(solution)/shard_map/pallas_call | solution.py:386
  31.0 0.7 %copy.7 = bf16[128,1024]{1,0:T(8,128)(2,1)} copy(bf16[128,1024]{1,0:T(8,128)(2,1)S(1)} %shard_map.55) | data formatting | bytes 524288

commit v6 on v3

--- a/solution.py
+++ b/solution.py
@@ -11,7 +11,7 @@
 HQ = 32
 KVH = 8
 HD = 128
-PART = 2 * HD
+PART = 4 * HD
 MESH = pl.DeviceIdType.MESH
 
 
@@ -129,12 +129,12 @@
             device_id_type=MESH,
         )
 
-    def send_q(p):
-        for d in range(n - 1, 0, -1):
-            for direction in (0, 1):
-
-                @pl.when(receives(1 - direction, d))
-                def _():
+    def send_q(d):
+        for direction in (0, 1):
+
+            @pl.when(receives(1 - direction, d))
+            def _():
+                for p in range(parts):
                     q_copy(direction, d, p).start()
 
     pl.semaphore_wait(barrier, n - 1)
@@ -162,16 +162,12 @@
 
     for p in range(parts):
         pack_q(p)
-        if p == 0:
-            send_q(0)
-    sent = 1
+    for d in range(n - 1, 1, -1):
+        send_q(d)
     for d in range(1, n - 1):
         pass_on(d)
-        if sent < parts:
-            send_q(sent)
-            sent += 1
-    for p in range(sent, parts):
-        send_q(p)
+        if d == 1:
+            send_q(1)
 
     local = lax.broadcasted_iota(jnp.int32, (tok, tok), 0)
     lane = lax.broadcasted_iota(jnp.int32, (1, tok), 1)

time: 29.4 us -> 28.7 us (0.976)
  Pallas kernels: 28.5 us -> 27.8 us
    pallas_call x1, Pallas kernels: 28.5 us -> 27.8 us  [body(): pl.pallas_call(functools.partial(kernel, n), out_shape=pltpu.VMEM((tok, w...]
where the time goes in v6:
time: 28.7 us; the launch traced here: 28.5 us
  Pallas kernels  27.8 us (97%)
  local copies, waits for them, and re-layouts  0.71 us (2%)
    pallas_call x1, Pallas kernels, body(): pl.pallas_call(functools.partial(kernel, n), out_shape=pltpu.VMEM((tok, w...  27.8 us
    unnamed x1, local copies, waits for them, and re-layouts  0.71 us

profile of v6, /device:TPU:0, one launch (start us, length us, event | category | flops | bytes accessed | tf_op | source)
XLA Modules:
  0.0 28.5 jit_solution(12356252558278637770)
XLA Ops:
  0.0 27.8 %shard_map.55 = bf16[128,1024]{1,0:T(8,128)(2,1)S(1)} custom-call(s32[4,4]{1,0:T(4,128)} %counts_in.1, s32[16]{0:T(128)} %docs_in.1, bf16[128,1024]{1,0:T(8,128)(2,1)} %q_in.1, bf16[128,256]{1,0:T(8,128)(2,1)} %k_in.1, bf16[128,256]{1,0:T(8,128)(2,1)} %v_in.1), custom_call_target="tpu_custom_call" | custom-call | tf_op jit(solution)/shard_map/pallas_call | solution.py:278
  27.8 0.7 %copy.7 = bf16[128,1024]{1,0:T(8,128)(2,1)} copy(bf16[128,1024]{1,0:T(8,128)(2,1)S(1)} %shard_map.55) | data formatting | bytes 524288
